TPU v7x, 32 devices: a whole 2x2x4 slice. The times are simulated.
32 devices in a mesh: wide: 8 (over y, x, core), narrow: 4 (over z).
Axes of the slice: x: 2, y: 2, z: 4, core: 2. Of those that a mesh axis runs over, the one named last changes fastest.
Arguments:
- embeds: bfloat16 [8192, 768], P(('wide', 'narrow')), may hold values from -6 to 6
- skip_tokens: bfloat16 [8192, 768], P(('wide', 'narrow')), may hold values from -6 to 6
- cotangent: bfloat16 [8192, 768], P(('wide', 'narrow')), may hold values from -6 to 6
- lengths: int32 [64], P(('wide', 'narrow')), may hold values from 32 to 128, as said below
- qkv_weight: float32 [2, 768, 2304], P(None, ('wide', 'narrow')), may hold values from -0.21875 to 0.21875
- out_weight: float32 [2, 768, 768], P(None, ('wide', 'narrow')), may hold values from -0.625 to 0.625
- up_weight: float32 [2, 768, 3072], P(None, ('wide', 'narrow')), may hold values from -0.21875 to 0.21875
- down_weight: float32 [2, 3072, 768], P(None, ('wide', 'narrow')), may hold values from -0.109375 to 0.109375
- up_bias: float32 [2, 3072], P(None, ('wide', 'narrow')), may hold values from -2 to 2
- norm_gains: float32 [2, 2, 768], P(None, None, ('wide', 'narrow')), may hold values from 0.5 to 1.5
- biases: float32 [2, 6, 768], P(None, None, ('wide', 'narrow')), may hold values from -2 to 2
- qkv_moments: float32 [2, 2, 768, 2304], P(None, None, ('wide', 'narrow')), as said below
- out_moments: float32 [2, 2, 768, 768], P(None, None, ('wide', 'narrow')), as said below
- up_moments: float32 [2, 2, 768, 3072], P(None, None, ('wide', 'narrow')), as said below
- down_moments: float32 [2, 2, 3072, 768], P(None, None, ('wide', 'narrow')), as said below
- up_bias_moments: float32 [2, 2, 3072], P(None, None, ('wide', 'narrow')), as said below
- gain_moments: float32 [2, 2, 2, 768], P(None, None, None, ('wide', 'narrow')), as said below
- bias_moments: float32 [2, 2, 6, 768], P(None, None, None, ('wide', 'narrow')), as said below
Outputs:
- head_output: bfloat16 [8192, 768], P(('wide', 'narrow'))
- embeds_grad: float32 [8192, 768], P(('wide', 'narrow'))
- skip_grad: float32 [8192, 768], P(('wide', 'narrow'))
- qkv_weight_step: float32 [2, 768, 2304], P(None, ('wide', 'narrow'))
- out_weight_step: float32 [2, 768, 768], P(None, ('wide', 'narrow'))
- up_weight_step: float32 [2, 768, 3072], P(None, ('wide', 'narrow'))
- down_weight_step: float32 [2, 3072, 768], P(None, ('wide', 'narrow'))
- up_bias_step: float32 [2, 3072], P(None, ('wide', 'narrow'))
- norm_gains_step: float32 [2, 2, 768], P(None, None, ('wide', 'narrow'))
- biases_step: float32 [2, 6, 768], P(None, None, ('wide', 'narrow'))
- qkv_moments_new: float32 [2, 2, 768, 2304], P(None, None, ('wide', 'narrow'))
- out_moments_new: float32 [2, 2, 768, 768], P(None, None, ('wide', 'narrow'))
- up_moments_new: float32 [2, 2, 768, 3072], P(None, None, ('wide', 'narrow'))
- down_moments_new: float32 [2, 2, 3072, 768], P(None, None, ('wide', 'narrow'))
- up_bias_moments_new: float32 [2, 2, 3072], P(None, None, ('wide', 'narrow'))
- gain_moments_new: float32 [2, 2, 2, 768], P(None, None, None, ('wide', 'narrow'))
- bias_moments_new: float32 [2, 2, 6, 768], P(None, None, None, ('wide', 'narrow'))
Inputs may be any that keep to these rules, and one draw needn't show every extreme that they name: `lengths`: positions at or past a span's length are padding; some span has length exactly 32 and some exactly 128. `qkv_moments`: index 0 of the first dimension holds first moments, index 1 second moments, which are positive. `out_moments`: index 0 of the first dimension holds first moments, index 1 second moments, which are positive. `up_moments`: index 0 of the first dimension holds first moments, index 1 second moments, which are positive. `down_moments`: index 0 of the first dimension holds first moments, index 1 second moments, which are positive. `up_bias_moments`: index 0 of the first dimension holds first moments, index 1 second moments, which are positive. `gain_moments`: index 0 of the first dimension holds first moments, index 1 second moments, which are positive. `bias_moments`: index 0 of the first dimension holds first moments, index 1 second moments, which are positive.
All inputs are finite; a program needn't handle non-finite values.
Results may differ from a plain program's by a relative error of at most 0.02.
Values may be sent and summed in bfloat16 or wider, within the bound.
A program may use at most 256 MiB of HBM per device.

v0:
```python
import math

import jax
import jax.numpy as jnp
from jax import lax
from jax.experimental import pallas as pl
from jax.experimental.pallas import tpu as pltpu
from jax.sharding import PartitionSpec as P

HEADS = 12
SPAN = 128

norm_epsilon = 1e-12
score_scale = 0.125
masked_score = -1000000000.0
beta_first = 0.9
beta_second = 0.999
adam_epsilon = 1e-08
weight_decay = 0.01
first_fix = 1.0 - 0.9**10
second_fix = 1.0 - 0.999**10


def dot_first(left_side, right_side):
    return lax.dot_general(
        left_side, right_side, (((0,), (0,)), ((), ())), preferred_element_type=jnp.float32
    )


def dot_last(left_side, right_side):
    return lax.dot_general(
        left_side, right_side, (((1,), (1,)), ((), ())), preferred_element_type=jnp.float32
    )


def normalize(values, gain_row, shift_row):
    centred = values - jnp.mean(values, axis=-1, keepdims=True)
    inv_scale = lax.rsqrt(jnp.mean(centred * centred, axis=-1, keepdims=True) + norm_epsilon)
    normed = centred * inv_scale
    return (normed * gain_row + shift_row, normed, inv_scale)


def normalize_back(gradient, normed, inv_scale, gain_row):
    grad_gain = jnp.sum(gradient * normed, axis=0)
    grad_shift = jnp.sum(gradient, axis=0)
    scaled = gradient * gain_row
    grad_in = inv_scale * (
        scaled
        - jnp.mean(scaled, axis=-1, keepdims=True)
        - normed * jnp.mean(scaled * normed, axis=-1, keepdims=True)
    )
    return (grad_in, grad_gain, grad_shift)


def head_view(tensor):
    return tensor.reshape(tensor.shape[0] // SPAN, SPAN, HEADS, tensor.shape[1] // HEADS)


def attend_scores(queries, keys_low, key_valid):
    scores = (
        jnp.einsum(
            "bqhe,bkhe->bhqk",
            head_view(queries),
            head_view(keys_low),
            preferred_element_type=jnp.float32,
        )
        * score_scale
    )
    return jnp.where(key_valid[:, None, None, :], scores, masked_score)


def forward_block(weights, inputs, key_valid):
    qkv_w, out_w, up_w, down_w, up_b, gain_rows, biases = weights
    gains_wide = gain_rows.astype(jnp.float32)
    biases_wide = biases.astype(jnp.float32)
    row_count, model_width = inputs.shape
    mixed_in = jnp.dot(inputs, qkv_w, preferred_element_type=jnp.float32)
    queries = (mixed_in[:, :model_width] + biases_wide[0]).astype(jnp.bfloat16)
    keys_low = mixed_in[:, model_width : 2 * model_width].astype(jnp.bfloat16)
    values_low = (mixed_in[:, 2 * model_width :] + biases_wide[1]).astype(jnp.bfloat16)
    scores = attend_scores(queries, keys_low, key_valid)
    row_max = jnp.max(scores, axis=-1, keepdims=True)
    weights_exp = jnp.exp(scores - row_max)
    row_total = jnp.sum(weights_exp, axis=-1, keepdims=True)
    softmax_out = (weights_exp / row_total).astype(jnp.bfloat16)
    log_total = row_max + jnp.log(row_total)
    context = jnp.einsum(
        "bhqk,bkhe->bqhe", softmax_out, head_view(values_low), preferred_element_type=jnp.float32
    )
    context = context.reshape(row_count, model_width).astype(jnp.bfloat16)
    attended = jnp.dot(context, out_w, preferred_element_type=jnp.float32) + biases_wide[2]
    hidden, normed_one, scale_one = normalize(
        inputs.astype(jnp.float32) + attended, gains_wide[0], biases_wide[3]
    )
    hidden_low = hidden.astype(jnp.bfloat16)
    pre_gelu = jnp.dot(hidden_low, up_w, preferred_element_type=jnp.float32) + up_b.astype(
        jnp.float32
    )
    activated = jax.nn.gelu(pre_gelu, approximate=False).astype(jnp.bfloat16)
    branch_out = jnp.dot(activated, down_w, preferred_element_type=jnp.float32) + biases_wide[4]
    output, normed_two, scale_two = normalize(hidden + branch_out, gains_wide[1], biases_wide[5])
    saved = (
        queries,
        keys_low,
        values_low,
        log_total,
        context,
        normed_one,
        scale_one,
        hidden_low,
        pre_gelu,
        activated,
        normed_two,
        scale_two,
    )
    return (output, saved)


def backward_block(weights, inputs, key_valid, grad_out):
    qkv_w, out_w, up_w, down_w, up_b, gain_rows, biases = weights
    gains_wide = gain_rows.astype(jnp.float32)
    row_count, model_width = inputs.shape
    output, saved = forward_block(weights, inputs, key_valid)
    (
        queries,
        keys_low,
        values_low,
        log_total,
        context,
        normed_one,
        scale_one,
        hidden_low,
        pre_gelu,
        activated,
        normed_two,
        scale_two,
    ) = saved
    grad_pre_two, grad_gain_two, grad_shift_two = normalize_back(
        grad_out, normed_two, scale_two, gains_wide[1]
    )
    grad_branch = grad_pre_two.astype(jnp.bfloat16)
    grad_down_w = dot_first(activated, grad_branch)
    grad_act = dot_last(grad_branch, down_w)
    _, gelu_back = jax.vjp(lambda inner: jax.nn.gelu(inner, approximate=False), pre_gelu)
    grad_pre_gelu = gelu_back(grad_act)[0].astype(jnp.bfloat16)
    grad_up_w = dot_first(hidden_low, grad_pre_gelu)
    grad_hidden = grad_pre_two + dot_last(grad_pre_gelu, up_w)
    grad_pre_one, grad_gain_one, grad_shift_one = normalize_back(
        grad_hidden, normed_one, scale_one, gains_wide[0]
    )
    grad_attended = grad_pre_one.astype(jnp.bfloat16)
    grad_out_w = dot_first(context, grad_attended)
    grad_context = head_view(dot_last(grad_attended, out_w).astype(jnp.bfloat16))
    scores = attend_scores(queries, keys_low, key_valid)
    softmax_full = jnp.exp(scores - log_total)
    grad_probs = jnp.einsum(
        "bqhe,bkhe->bhqk", grad_context, head_view(values_low), preferred_element_type=jnp.float32
    )
    grad_values = jnp.einsum(
        "bhqk,bqhe->bkhe",
        softmax_full.astype(jnp.bfloat16),
        grad_context,
        preferred_element_type=jnp.float32,
    )
    grad_values = grad_values.reshape(row_count, model_width).astype(jnp.bfloat16)
    grad_scores = softmax_full * (
        grad_probs - jnp.sum(softmax_full * grad_probs, axis=-1, keepdims=True)
    )
    grad_scores = grad_scores.astype(jnp.bfloat16)
    grad_queries = (
        jnp.einsum(
            "bhqk,bkhe->bqhe", grad_scores, head_view(keys_low), preferred_element_type=jnp.float32
        )
        * score_scale
    )
    grad_queries = grad_queries.reshape(row_count, model_width).astype(jnp.bfloat16)
    grad_keys = (
        jnp.einsum(
            "bhqk,bqhe->bkhe", grad_scores, head_view(queries), preferred_element_type=jnp.float32
        )
        * score_scale
    )
    grad_keys = grad_keys.reshape(row_count, model_width).astype(jnp.bfloat16)
    grad_mixed = jnp.concatenate([grad_queries, grad_keys, grad_values], axis=1)
    grad_qkv_w = dot_first(inputs, grad_mixed)
    grad_inputs = grad_pre_one + dot_last(grad_mixed, qkv_w)
    grad_gains = jnp.stack([grad_gain_one, grad_gain_two])
    grad_biases = jnp.stack(
        [
            jnp.sum(grad_queries, axis=0, dtype=jnp.float32),
            jnp.sum(grad_values, axis=0, dtype=jnp.float32),
            jnp.sum(grad_attended, axis=0, dtype=jnp.float32),
            grad_shift_one,
            jnp.sum(grad_branch, axis=0, dtype=jnp.float32),
            grad_shift_two,
        ]
    )
    grads = (
        grad_qkv_w,
        grad_out_w,
        grad_up_w,
        grad_down_w,
        jnp.sum(grad_pre_gelu, axis=0, dtype=jnp.float32),
        grad_gains,
        grad_biases,
    )
    return (output, grad_inputs, grads)


MESH = pl.DeviceIdType.MESH


class Refs:
    def __init__(self, **refs):
        for name, ref in refs.items():
            setattr(self, name, ref)


def place():
    wide = lax.axis_index("wide")
    z = lax.axis_index("narrow")
    return wide // 4, (wide // 2) % 2, wide % 2, z


def device(y, x, c, z):
    return ((y * 2 + x) * 2 + c, z)


def flat(y, x, c, z):
    return ((y * 2 + x) * 2 + c) * 4 + z


def near(z, k):
    if k == 0:
        return z
    if k == 1:
        return z + 1 - 2 * (z % 2)
    if k == 2:
        return (z + 2) % 4
    return 3 - z


def greet(wide, z):
    barrier = pltpu.get_barrier_semaphore()
    for k in range(1, 8):
        pl.semaphore_signal(barrier, inc=1, device_id=((wide + k) % 8, z), device_id_type=MESH)

    @pl.when(z < 3)
    def _():
        pl.semaphore_signal(barrier, inc=1, device_id=(wide, z + 1), device_id_type=MESH)

    @pl.when(z > 0)
    def _():
        pl.semaphore_signal(barrier, inc=1, device_id=(wide, z - 1), device_id_type=MESH)

    pl.semaphore_wait(barrier, 8 + ((z + 1) // 2) % 2)


def run_if(pred, action):
    if pred is None:
        action()
    else:
        pl.when(pred)(action)


def send(src, dst, send_sem, recv_sem, there, pred=None):
    run_if(
        pred,
        lambda: pltpu.make_async_remote_copy(
            src_ref=src, dst_ref=dst, send_sem=send_sem, recv_sem=recv_sem, device_id=there, device_id_type=MESH
        ).start(),
    )


def bytes_of(ref, sem):
    me = (lax.axis_index("wide"), lax.axis_index("narrow"))
    return pltpu.make_async_remote_copy(
        src_ref=ref, dst_ref=ref, send_sem=sem, recv_sem=sem, device_id=me, device_id_type=MESH
    )


def await_bytes(ref, sem, pred=None):
    run_if(pred, lambda: bytes_of(ref, sem).wait_recv())


def await_sent(ref, sem, pred=None):
    run_if(pred, lambda: bytes_of(ref, sem).wait_send())


def await_column_sends(many, each, sem, z):
    await_sent(many(each), sem, (z == 0) | (z == 3))
    await_sent(many(5 * each), sem, (z == 1) | (z == 2))


def column_steps(slabs, manys, sem):
    y, x, c, z = place()
    up, down = device(y, x, c, z + 1), device(y, x, c, z - 1)

    def push(i, slab, zz, there, pred):
        send(slab(zz), slab(zz), sem.at[i, 4], sem.at[i, zz], there, pred)

    def own():
        for i, slab in enumerate(slabs):
            push(i, slab, z, up, z < 3)
            push(i, slab, z, down, z > 0)

    def take(dist):
        for i, slab in enumerate(slabs):
            low, high = z - dist, z + dist
            await_bytes(slab(low), sem.at[i, low], z >= dist)
            if dist < 3:
                push(i, slab, low, up, (z >= dist) & (z < 3))
            await_bytes(slab(high), sem.at[i, high], z <= 3 - dist)
            if dist < 3:
                push(i, slab, high, down, (z <= 3 - dist) & (z > 0))

    def drain():
        for i, many in enumerate(manys):
            await_column_sends(many, 1, sem.at[i, 4], z)

    return [own] + [lambda dist=dist: take(dist) for dist in (1, 2, 3)], drain


GATHER_SEMS = 21


def gather_steps(subs, many, sem):
    y, x, c, z = place()
    each = len(subs)
    sib = device(y, x, 1 - c, z)
    xn = device(y, 1 - x, c, z)
    yn = device(1 - y, x, c, z)
    mine = flat(y, x, c, z)

    def unit(sub, far1, far2, zz, core):
        fx, fy = (far1, far2) if sub[2] == "x" else (far2, far1)
        return flat(1 - y if fy else y, 1 - x if fx else x, core, zz)

    def push(sub, at, send_at, role, target, pred=None, src=None):
        send(sub[1](at) if src is None else src, sub[1](at), sem.at[send_at], sem.at[role], target, pred)

    def along(sub, at, up, role, pred, src=None):
        push(sub, at, 17, role, device(y, x, c, z + 1 if up else z - 1), pred, src)

    def first(sub, at, zz, pred=None, src=None):
        push(sub, at, 18, 4 + zz, xn if sub[2] == "x" else yn, pred, src)

    def second(sub, at, far, zz, pred=None, src=None):
        push(sub, at, 19, 8 + 4 * far + zz, yn if sub[2] == "x" else xn, pred, src)

    def sibling(sub, at, pred=None, src=None):
        push(sub, at, 20, 16, sib, pred, src)

    def own():
        for sub in subs:
            along(sub, mine, True, z, z < 3, sub[0])
            along(sub, mine, False, z, z > 0, sub[0])
        for sub in subs:
            first(sub, mine, z, None, sub[0])
            second(sub, mine, 0, z, None, sub[0])
        for sub in subs:
            sibling(sub, mine, None, sub[0])

    def from_z(dist):
        for up in (True, False):
            zz = z - dist if up else z + dist
            have = (z >= dist) if up else (z <= 3 - dist)
            at = flat(y, x, c, zz)

            @pl.when(have)
            def _(up=up, zz=zz, at=at):
                await_bytes(many(each), sem.at[zz])
                for sub in subs:
                    if dist < 3:
                        along(sub, at, up, zz, (z < 3) if up else (z > 0))
                for sub in subs:
                    first(sub, at, zz)
                    second(sub, at, 0, zz)
                    sibling(sub, at)

    def from_first(k):
        zz = near(z, k)
        await_bytes(many(each), sem.at[4 + zz])
        for sub in subs:
            at = unit(sub, True, False, zz, c)
            second(sub, at, 1, zz)
            sibling(sub, at)

    def from_second(far, k):
        zz = near(z, k)
        await_bytes(many(each), sem.at[8 + 4 * far + zz])
        for sub in subs:
            sibling(sub, unit(sub, far == 1, True, zz, c))

    def finish():
        await_bytes(many(16 * each), sem.at[16])

    def drain():
        await_column_sends(many, each, sem.at[17], z)
        await_sent(many(4 * each), sem.at[18])
        await_sent(many(8 * each), sem.at[19])
        await_sent(many(16 * each), sem.at[20])

    steps = [own, lambda: from_z(1), lambda: from_first(0), lambda: from_z(2), lambda: from_first(1)]
    steps += [lambda: from_z(3), lambda: (from_first(2), from_first(3))]
    for far in range(2):
        steps += [lambda far=far, k=k: from_second(far, k) for k in range(4)]
    return steps + [finish], drain


REDUCE_SEMS = 33
TARGETS = (0, 3, 1, 2)


class Reduce:
    def __init__(self, subs, sem):
        self.subs, self.sem, self.each = subs, sem, len(subs)
        self.y, self.x, self.c, self.z = place()
        y, x, c, z = self.y, self.x, self.c, self.z
        self.sib = device(y, x, 1 - c, z)
        self.xn, self.yn = device(y, 1 - x, c, z), device(1 - y, x, c, z)

    def own(self, sub, far1, far2, zz, core):
        fx, fy = (far1, far2) if sub.dim == "x" else (far2, far1)
        cy, cx = (1 - self.y if fy else self.y), (1 - self.x if fx else self.x)
        return sub.own(flat(cy, cx, core, zz)), (cy * 2 + cx) * 4 + zz

    def coord(self, sub, far):
        here = self.x if sub.dim == "x" else self.y
        return 1 - here if far else here

    def take(self, at, buffer, count=1):
        await_bytes(buffer.at[pl.ds(0, count * self.each)], self.sem.at[at])

    def add(self, dst, *parts):
        total = dst[...].astype(jnp.float32)
        for part in parts:
            total = total + part[...].astype(jnp.float32)
        dst[...] = total.astype(dst.dtype)

    def start(self, zz):
        for far1, far2 in ((False, True), (True, True), (True, False), (False, False)):
            at = 6 * zz + (0 if far2 else 1 if far1 else 2)
            for sub in self.subs:
                src, slot = self.own(sub, far1, far2, zz, 1 - self.c)
                send(src, sub.sib.at[slot], self.sem.at[29], self.sem.at[at], self.sib)

    def start_chip(self, chip):
        cy, cx = chip // 2, chip % 2
        for zz in TARGETS:
            for sub in self.subs:
                fy, fx = (cy + self.y) % 2, (cx + self.x) % 2
                far1, far2 = (fx, fy) if sub.dim == "x" else (fy, fx)
                at = 6 * zz + (1 - far2) * (2 - far1)
                src = sub.own(flat(cy, cx, 1 - self.c, zz))
                send(src, sub.sib.at[chip * 4 + zz], self.sem.at[29], self.sem.at[at], self.sib)

    def step_a(self, zz):
        self.take(6 * zz, self.subs[0].sib, 2)
        for far1 in (False, True):
            for sub in self.subs:
                acc, slot = self.own(sub, far1, True, zz, self.c)
                self.add(acc, sub.sib.at[slot])
                slot = self.coord(sub, far1) * 4 + zz
                there = self.yn if sub.dim == "x" else self.xn
                send(acc, sub.second.at[slot], self.sem.at[30], self.sem.at[6 * zz + (3 if far1 else 4)], there)

    def step_b(self, zz):
        self.take(6 * zz + 1, self.subs[0].sib)
        self.take(6 * zz + 3, self.subs[0].second)
        for sub in self.subs:
            acc, slot = self.own(sub, True, False, zz, self.c)
            self.add(acc, sub.sib.at[slot], sub.second.at[self.coord(sub, True) * 4 + zz])
            there = self.xn if sub.dim == "x" else self.yn
            send(acc, sub.first.at[zz], self.sem.at[31], self.sem.at[6 * zz + 5], there)

    def chain(self, sub, acc, zz, up, pred):
        z = self.z
        slot = zz if up else jnp.where(z - 1 == zz, 4, zz)
        there = device(self.y, self.x, self.c, z + 1 if up else z - 1)
        send(acc, sub.chain.at[slot], self.sem.at[32], self.sem.at[24 + slot], there, pred)

    def step_c(self, zz):
        self.take(6 * zz + 2, self.subs[0].sib)
        self.take(6 * zz + 4, self.subs[0].second)
        self.take(6 * zz + 5, self.subs[0].first)
        for sub in self.subs:
            acc, slot = self.own(sub, False, False, zz, self.c)
            self.add(acc, sub.sib.at[slot], sub.second.at[self.coord(sub, False) * 4 + zz], sub.first.at[zz])
            if zz > 0:
                self.chain(sub, acc, zz, True, self.z == 0)
            if zz < 3:
                self.chain(sub, acc, zz, False, self.z == 3)

    def relay(self, zz, at, up):
        @pl.when(self.z == at)
        def _():
            self.take(24 + zz, self.subs[0].chain)
            for sub in self.subs:
                acc, _ = self.own(sub, False, False, zz, self.c)
                self.add(acc, sub.chain.at[zz])
                self.chain(sub, acc, zz, up, None)

    def step_d(self, zz):
        if zz >= 2:
            self.relay(zz, 1, True)
        else:
            self.relay(zz, 2, False)

    def step_e(self, zz):
        if zz == 3:
            self.relay(zz, 2, True)
        if zz == 0:
            self.relay(zz, 1, False)

    def finish(self):
        z = self.z
        for sub in self.subs:
            acc, _ = self.own(sub, False, False, z, self.c)
            sub.out[...] = acc[...].astype(jnp.float32)
        for pred, slot in ((z > 0, z), (z < 3, 4)):

            @pl.when(pred)
            def _(slot=slot):
                self.take(24 + slot, self.subs[0].chain)
                for sub in self.subs:
                    sub.out[...] += sub.chain[slot].astype(jnp.float32)

        for at, count in ((29, 16), (30, 8), (31, 4), (32, 3)):
            await_sent(self.subs[0].all.at[pl.ds(0, count * self.each)], self.sem.at[at])


class Waves:
    def __init__(self, groups, lags):
        self.waves = [(made, zz) for made in groups for zz in TARGETS]
        self.lags = lags
        self.at = 0

    def step(self):
        stages = (Reduce.step_a, Reduce.step_b, Reduce.step_c, Reduce.step_d, Reduce.step_e)
        for lag, stage in zip(self.lags, stages):
            k = self.at - lag
            if 0 <= k < len(self.waves):
                group, zz = self.waves[k]
                for made in group:
                    stage(made, zz)
        k = self.at - self.lags[-1] - 1
        if 0 <= k < len(self.waves) and k % 4 == 3:
            for made in self.waves[k][0]:
                made.finish()
        self.at += 1

    def left(self):
        return len(self.waves) + self.lags[-1] + 1 - self.at


def erf_of(v):
    return lax.erf(v)


def mm(a, b):
    return jnp.dot(a, b, preferred_element_type=jnp.float32)


def mm_nt(a, b):
    return lax.dot_general(a, b, (((1,), (1,)), ((), ())), preferred_element_type=jnp.float32)


def mm_tn(a, b):
    return lax.dot_general(a, b, (((0,), (0,)), ((), ())), preferred_element_type=jnp.float32)


def columns(ref, start, stop):
    block = ref[:, :, start:stop]
    return block.reshape(block.shape[0] * block.shape[1], stop - start)


def rows_of(ref, start, stop):
    block = ref[start:stop]
    return block.reshape(block.shape[0] * block.shape[1], block.shape[2])


def put_columns(ref, start, values):
    owners, share = ref.shape[0], ref.shape[1]
    ref[:, :, start : start + values.shape[1]] = values.astype(ref.dtype).reshape(
        owners, share, values.shape[1]
    )


def norm_rows(values):
    centred = values - jnp.mean(values, axis=-1, keepdims=True)
    inv_scale = lax.rsqrt(jnp.mean(centred * centred, axis=-1, keepdims=True) + norm_epsilon)
    return centred * inv_scale, inv_scale


def norm_rows_back(gradient, normed, inv_scale, gain_row):
    scaled = gradient * gain_row
    return inv_scale * (
        scaled
        - jnp.mean(scaled, axis=-1, keepdims=True)
        - normed * jnp.mean(scaled * normed, axis=-1, keepdims=True)
    )


def column_sum(values):
    return jnp.sum(values.astype(jnp.float32), axis=0, keepdims=True)


def head_forward(s, w1, w2, small, lengths):
    width = s.x.shape[1]
    spans = s.x.shape[0] // SPAN
    x = s.x[...]
    s.q[...] = (mm(x, columns(w1, 0, width)) + small(2)).astype(jnp.bfloat16)
    s.k[...] = mm(x, columns(w1, width, 2 * width)).astype(jnp.bfloat16)
    s.v[...] = (mm(x, columns(w1, 2 * width, 3 * width)) + small(3)).astype(jnp.bfloat16)
    yield
    lane = lax.broadcasted_iota(jnp.int32, (SPAN, 128), 1)
    for span in range(spans):
        keep = lax.broadcasted_iota(jnp.int32, (SPAN, 128), 1) < lengths[span]
        for pair in range(width // 128):
            at = (slice(span * SPAN, (span + 1) * SPAN), slice(pair * 128, (pair + 1) * 128))
            q, k, v = s.q[at], s.k[at], s.v[at]
            parts = []
            for side in range(2):
                here = (lane < 64) if side == 0 else (lane >= 64)
                scores = mm_nt(jnp.where(here, q, jnp.zeros_like(q)), k) * score_scale
                scores = jnp.where(keep, scores, masked_score)
                weight = jnp.exp(scores - jnp.max(scores, axis=-1, keepdims=True))
                probs = weight / jnp.sum(weight, axis=-1, keepdims=True)
                s.p[(span * 6 + pair) * 2 + side] = probs
                parts.append(mm(probs.astype(jnp.bfloat16), v))
            s.ctx[at] = jnp.where(lane < 64, parts[0], parts[1]).astype(jnp.bfloat16)
        yield
    attended = mm(s.ctx[...], columns(w1, 3 * width, 4 * width)) + small(4)
    normed, inv_scale = norm_rows(s.x[...].astype(jnp.float32) + attended)
    s.n1[...] = normed
    s.r1[...] = inv_scale
    hidden = normed * small(0) + small(5)
    s.h[...] = hidden
    s.hl[...] = hidden.astype(jnp.bfloat16)
    yield
    for part in range(4):
        pre = mm(s.hl[...], columns(w1, (4 + part) * width, (5 + part) * width)) + small(8 + part)
        half_erf = 0.5 + 0.5 * erf_of(pre * (0.5**0.5))
        s.g[part] = (pre * half_erf).astype(jnp.bfloat16)
        s.gp[part] = half_erf + pre * (jnp.exp(-0.5 * pre * pre) * (0.5 / math.pi) ** 0.5)
        yield
    branch = small(6)
    share = w2.shape[0] // 4
    for part in range(4):
        branch = branch + mm(s.g[part], rows_of(w2, part * share, (part + 1) * share))
    normed, inv_scale = norm_rows(s.h[...] + branch)
    s.n2[...] = normed
    s.r2[...] = inv_scale
    s.y[...] = (normed * small(1) + small(7)).astype(jnp.bfloat16)
    yield


def head_backward(s, w1, w2, g1, g2, small, sums, grad_in):
    width = s.x.shape[1]
    spans = s.x.shape[0] // SPAN
    grad_out = s.cot[...].astype(jnp.float32)
    sums[1:2] = column_sum(grad_out * s.n2[...])
    sums[7:8] = column_sum(grad_out)
    pre_two = norm_rows_back(grad_out, s.n2[...], s.r2[...], small(1))
    s.h[...] = pre_two
    branch = pre_two.astype(jnp.bfloat16)
    s.dz[...] = branch
    sums[6:7] = column_sum(branch)
    yield
    owners = w2.shape[0]
    share = owners // 4
    for part in range(4):
        own = slice(part * share, (part + 1) * share)
        grad_act = mm_nt(s.dz[...], rows_of(w2, part * share, (part + 1) * share))
        grad_pre = (grad_act * s.gp[part]).astype(jnp.bfloat16)
        g2[own] = (
            mm_tn(s.g[part], s.dz[...]).astype(jnp.bfloat16).reshape(share, g2.shape[1], width)
        )
        s.g[part] = grad_pre
        sums[8 + part : 9 + part] = column_sum(grad_pre)
        yield
    for part in range(4):
        at = (4 + part) * width
        grad_pre = s.g[part]
        s.h[...] += mm_nt(grad_pre, columns(w1, at, at + width))
        put_columns(g1, at, mm_tn(s.hl[...], grad_pre))
        yield
    grad_hidden = s.h[...]
    sums[0:1] = column_sum(grad_hidden * s.n1[...])
    sums[5:6] = column_sum(grad_hidden)
    pre_one = norm_rows_back(grad_hidden, s.n1[...], s.r1[...], small(0))
    s.h[...] = pre_one
    attended = pre_one.astype(jnp.bfloat16)
    s.dz[...] = attended
    sums[4:5] = column_sum(attended)
    yield
    s.hl[...] = mm_nt(attended, columns(w1, 3 * width, 4 * width)).astype(jnp.bfloat16)
    put_columns(g1, 3 * width, mm_tn(s.ctx[...], attended))
    yield
    lane = lax.broadcasted_iota(jnp.int32, (SPAN, 128), 1)
    for span in range(spans):
        for pair in range(width // 128):
            at = (slice(span * SPAN, (span + 1) * SPAN), slice(pair * 128, (pair + 1) * 128))
            q, k, v, dc = s.q[at], s.k[at], s.v[at], s.hl[at]
            dq, dk, dv = [], [], []
            for side in range(2):
                here = (lane < 64) if side == 0 else (lane >= 64)
                probs = s.p[(span * 6 + pair) * 2 + side]
                grad_probs = mm_nt(jnp.where(here, dc, jnp.zeros_like(dc)), v)
                dv.append(mm_tn(probs.astype(jnp.bfloat16), dc))
                grad_scores = probs * (
                    grad_probs - jnp.sum(probs * grad_probs, axis=-1, keepdims=True)
                )
                grad_scores = grad_scores.astype(jnp.bfloat16)
                dq.append(mm(grad_scores, k))
                dk.append(mm_tn(grad_scores, q))
            join = lambda two: jnp.where(lane < 64, two[0], two[1])
            s.q[at] = (join(dq) * score_scale).astype(jnp.bfloat16)
            s.k[at] = (join(dk) * score_scale).astype(jnp.bfloat16)
            s.v[at] = join(dv).astype(jnp.bfloat16)
        yield
    sums[2:3] = column_sum(s.q[...])
    sums[3:4] = column_sum(s.v[...])
    total = s.h[...]
    for k, ref in enumerate((s.q, s.k, s.v)):
        total = total + mm_nt(ref[...], columns(w1, k * width, (k + 1) * width))
    grad_in[...] = total
    yield
    for k, ref in enumerate((s.q, s.k, s.v)):
        put_columns(g1, k * width, mm_tn(s.x[...], ref[...]))
    yield


HIGHEST = lax.Precision.HIGHEST
ROWS = 16


def iota(shape, axis):
    return lax.broadcasted_iota(jnp.int32, shape, axis)


def ones_where(condition, dtype):
    return jnp.where(condition, 1.0, 0.0).astype(dtype)


def exact(a, b, dims):
    return lax.dot_general(
        a, b, (dims, ((), ())), precision=HIGHEST, preferred_element_type=jnp.float32
    )


class Plane:
    def __init__(self, sem):
        self.sem = sem
        self.wide, self.z = lax.axis_index("wide"), lax.axis_index("narrow")
        self.sent = []

    def send(self, index, src, recv):
        for k in range(1, 8):
            peer = (self.wide + k) % 8
            send(src(peer), recv.at[self.wide], self.sem.at[index, 0], self.sem.at[index, 1], (peer, self.z))
        self.sent.append((index, recv))

    def arrive(self, index, recv):
        await_bytes(recv.at[pl.ds(0, 7)], self.sem.at[index, 1])

    def drain(self):
        for index, recv in self.sent:
            await_sent(recv.at[pl.ds(0, 7)], self.sem.at[index, 0])

    def total(self, index, recv):
        self.arrive(index, recv)
        total = recv[0].astype(jnp.float32)
        for k in range(1, 8):
            total = total + recv[k].astype(jnp.float32)
        return total

    def place_rows(self, two):
        row = iota((ROWS, two.shape[1]), 0)
        rows = jnp.where(row % 2 == 0, two[0:1], two[1:2])
        return jnp.where(row // 2 == self.wide, rows, 0.0)

    def pick_rows(self, values, first):
        row = iota(values.shape, 0)
        one = lambda k: jnp.sum(jnp.where(row == first + k, values, 0.0), axis=0, keepdims=True)
        return jnp.concatenate([one(0), one(1)], axis=0)

    def share(self, index, two, src, recv):
        placed = self.place_rows(two).astype(src.dtype)
        src[...] = placed
        recv[self.wide] = placed
        self.send(index, lambda peer: src, recv)

    def collect(self, index, values, src, recv):
        for k in range(2):
            src[k] = values[8 * k : 8 * k + 8]
        recv[self.wide] = jnp.where(self.wide // 4 == 0, values[0:8], values[8:16])
        self.send(index, lambda peer: src.at[peer // 4], recv)

    def collected(self, index, recv):
        return self.pick_rows(self.total(index, recv), 2 * (self.wide % 4))


def backbone_forward(s, plane, small, finish):
    x0, w0 = s.x0, s.w0
    width = x0.shape[1]
    spans = x0.shape[0] // SPAN
    wide = plane.wide
    x = x0[...]
    s.k0[...] = mm(x, columns(w0, width, 2 * width)).astype(jnp.bfloat16)
    s.v0[...] = (mm(x, columns(w0, 2 * width, 3 * width)) + small(3)).astype(jnp.bfloat16)
    first = jnp.concatenate(
        [x0[SPAN * span : SPAN * span + 1].astype(jnp.float32) for span in range(spans)], axis=0
    )
    query = mm(first.astype(jnp.bfloat16), columns(w0, 0, width)) + small(2)
    s.keep[0, 0:spans] = first
    s.keep[1, 0:spans] = query.astype(jnp.bfloat16).astype(jnp.float32)
    yield
    heads = ones_where(iota((width, 128), 0) // (width // HEADS) == iota((width, 128), 1), jnp.bfloat16)
    context = []
    for span in range(spans):
        at = slice(span * SPAN, (span + 1) * SPAN)
        product = s.k0[at].astype(jnp.float32) * s.keep[1, span : span + 1]
        scores = exact(product, heads.astype(jnp.float32), ((1,), (0,))) * score_scale
        scores = jnp.where(iota(scores.shape, 0) < s.lengths[span], scores, masked_score)
        weight = jnp.exp(scores - jnp.max(scores, axis=0, keepdims=True))
        probs = weight / jnp.sum(weight, axis=0, keepdims=True)
        s.p0[span] = probs
        spread = mm_nt(probs.astype(jnp.bfloat16), heads)
        context.append(jnp.sum(spread * s.v0[at].astype(jnp.float32), axis=0, keepdims=True))
    context = jnp.concatenate(context, axis=0).astype(jnp.bfloat16)
    s.keep[2, 0:spans] = context.astype(jnp.float32)
    attended = mm(context, columns(w0, 3 * width, 4 * width)) + small(4)
    normed, inv_scale = norm_rows(s.keep[0, 0:spans] + attended)
    hidden = normed * small(0) + small(5)
    s.keep[3, 0:spans] = normed
    s.keep[4, 0:spans] = jnp.broadcast_to(inv_scale, normed.shape)
    s.keep[5, 0:spans] = hidden
    plane.share(0, hidden, s.e0_src, s.e0)
    yield
    hidden_all = plane.total(0, s.e0).astype(jnp.bfloat16)
    share = width // 8
    pick = ones_where(iota((width, share), 0) == share * wide + iota((width, share), 1), jnp.bfloat16)
    own = mm(hidden_all, pick).astype(jnp.bfloat16)
    upz = s.upz
    part = upz.shape[2] // 8
    for k in range(8):
        s.e1_src[k] = mm(own, columns(upz, k * part, (k + 1) * part))
    s.e1[wide] = s.e1_src[wide]
    plane.send(1, lambda peer: s.e1_src.at[peer], s.e1)
    yield
    bias = jnp.where(wide % 2 == 0, small(8 + wide // 2)[:, :part], small(8 + wide // 2)[:, part:])
    pre = plane.total(1, s.e1) + bias
    half_erf = 0.5 + 0.5 * erf_of(pre * (0.5**0.5))
    s.g0[...] = (pre * half_erf).astype(jnp.bfloat16)
    s.gp0[...] = half_erf + pre * (jnp.exp(-0.5 * pre * pre) * (0.5 / math.pi) ** 0.5)
    plane.collect(2, mm(s.g0[...], rows_of(s.downz, 0, 4)), s.e2_src, s.e2)
    yield
    branch = plane.collected(2, s.e2) + small(6)
    normed, inv_scale = norm_rows(s.keep[5, 0:spans] + branch)
    s.keep[6, 0:spans] = normed
    s.keep[7, 0:spans] = jnp.broadcast_to(inv_scale, normed.shape)
    finish(normed * small(1) + small(7))
    yield


def backbone_backward(s, plane, small, grad_rows):
    x0, w0 = s.x0, s.w0
    width = x0.shape[1]
    spans = x0.shape[0] // SPAN
    wide = plane.wide
    keep = lambda k: s.keep[k, 0:spans]
    acts, sums = s.acts, s.sums0

    def put(item, values):
        for span in range(spans):
            row = span * ROWS + item
            acts[row : row + 1] = values[span : span + 1]

    acts[...] = jnp.zeros_like(acts)
    grad_out = grad_rows()
    sums[1:2] = column_sum(grad_out * keep(6))
    sums[7:8] = column_sum(grad_out)
    pre_two = norm_rows_back(grad_out, keep(6), keep(7), small(1))
    s.keep[8, 0:spans] = pre_two
    low = lambda a: a.astype(jnp.bfloat16).astype(jnp.float32)
    put(11, low(pre_two))
    plane.share(3, pre_two, s.e3_src, s.e3)
    yield
    branch = plane.total(3, s.e3).astype(jnp.bfloat16)
    grad_act = mm_nt(branch, rows_of(s.downz, 0, 4))
    part = s.g0.shape[1]
    s.e4_src[:, :part] = (grad_act * s.gp0[...]).astype(jnp.bfloat16)
    s.e4_src[:, part:] = s.g0[...]
    s.e4[wide] = s.e4_src[...]
    plane.send(4, lambda peer: s.e4_src, s.e4)
    yield
    plane.arrive(4, s.e4)
    total = jnp.zeros((ROWS, width // 8), jnp.float32)
    for k in range(8):
        both = s.e4[k]
        total = total + mm_nt(both[:, :part], columns(s.upz, k * part, (k + 1) * part))
        rows = plane.pick_rows(both.astype(jnp.float32), 2 * wide)
        at = slice((k % 2) * part, (k % 2 + 1) * part)
        for span in range(spans):
            row = span * ROWS + 3 + k // 2
            acts[row : row + 1, at] = rows[span : span + 1, :part]
            acts[row + 4 : row + 5, at] = rows[span : span + 1, part:]
    share = width // 8
    pick = ones_where(iota((width, share), 0) == share * wide + iota((width, share), 1), jnp.float32)
    plane.collect(5, exact(total, pick, ((1,), (1,))), s.e5_src, s.e5)
    yield
    grad_hidden = keep(8) + plane.collected(5, s.e5)
    sums[0:1] = column_sum(grad_hidden * keep(3))
    sums[5:6] = column_sum(grad_hidden)
    pre_one = norm_rows_back(grad_hidden, keep(3), keep(4), small(0))
    attended = pre_one.astype(jnp.bfloat16)
    context = low(mm_nt(attended, columns(w0, 3 * width, 4 * width)))
    heads = ones_where(iota((width, 128), 0) // (width // HEADS) == iota((width, 128), 1), jnp.bfloat16)
    queries = []
    for span in range(spans):
        at = slice(span * SPAN, (span + 1) * SPAN)
        probs = s.p0[span]
        grad_context = context[span : span + 1]
        product = s.v0[at].astype(jnp.float32) * grad_context
        grad_probs = exact(product, heads.astype(jnp.float32), ((1,), (0,)))
        grad_scores = probs * (grad_probs - jnp.sum(probs * grad_probs, axis=0, keepdims=True))
        spread = mm_nt(grad_scores.astype(jnp.bfloat16), heads) * score_scale
        queries.append(jnp.sum(spread * s.k0[at].astype(jnp.float32), axis=0, keepdims=True))
        s.k0[at] = (spread * s.keep[1, span : span + 1]).astype(jnp.bfloat16)
        s.v0[at] = (mm_nt(probs.astype(jnp.bfloat16), heads) * grad_context).astype(jnp.bfloat16)
    queries = jnp.concatenate(queries, axis=0).astype(jnp.bfloat16)
    sums[3:4] = column_sum(s.v0[...])
    put(0, keep(2))
    put(1, attended.astype(jnp.float32))
    put(2, low(keep(5)))
    put(12, keep(0))
    put(13, queries.astype(jnp.float32))
    s.acts_low[...] = acts[...].astype(jnp.bfloat16)
    s.keep[9, 0:spans] = pre_one + mm_nt(queries, columns(w0, 0, width))
    yield
    grad_in = s.embeds_grad
    grad_in[...] = mm_nt(s.k0[...], columns(w0, width, 2 * width))
    grad_in[...] += mm_nt(s.v0[...], columns(w0, 2 * width, 3 * width))
    for span in range(spans):
        grad_in[SPAN * span : SPAN * span + 1] += s.keep[9, span : span + 1]
    put_columns(w0, width, mm_tn(x0[...], s.k0[...]))
    put_columns(w0, 2 * width, mm_tn(x0[...], s.v0[...]))
    yield


def backbone_weight_grads(s, at, o1, o2, small_out):
    width = s.x0.shape[1]
    gathered = s.g[...].reshape(-1, width)
    spans = 64

    def item(k):
        shape = (spans, gathered.shape[0])
        row, column = iota(shape, 0), iota(shape, 1)
        pick = column == (row // 2) * 32 + (row % 2) * ROWS + k
        return mm(ones_where(pick, jnp.bfloat16), gathered)

    share = width // 32
    shape = (width, 128)

    def picker(count, offset, dtype):
        row, column = iota(shape, 0), iota(shape, 1)
        return ones_where((row + offset == count * at + column) & (column < count), dtype)

    narrow = picker(share, 0, jnp.bfloat16)
    own = lambda k: mm(item(k).astype(jnp.bfloat16), narrow).astype(jnp.bfloat16)
    grad_query = item(13)
    o1[0, :, 0:width] = mm_tn(own(12), grad_query.astype(jnp.bfloat16))[:share]
    grad_attended = item(1)
    o1[0, :, 3 * width : 4 * width] = mm_tn(own(0), grad_attended.astype(jnp.bfloat16))[:share]
    branch = item(11)
    hidden = own(2)
    wide_sum = jnp.zeros((1, 128), jnp.float32)
    act = jnp.zeros((spans, 128), jnp.float32)
    for part in range(4):
        grad_pre = item(3 + part)
        o1[0, :, (4 + part) * width : (5 + part) * width] = mm_tn(hidden, grad_pre.astype(jnp.bfloat16))[:share]
        act = act + mm(item(7 + part).astype(jnp.bfloat16), picker(4 * share, part * width, jnp.bfloat16))
        wide_sum = wide_sum + exact(
            column_sum(grad_pre), picker(4 * share, part * width, jnp.float32), ((1,), (0,))
        )
    o2[0] = mm_tn(act.astype(jnp.bfloat16), branch.astype(jnp.bfloat16))[: 4 * share]
    exact_narrow = picker(share, 0, jnp.float32)
    s.late[...] = jnp.zeros_like(s.late)
    for row, values in ((2, grad_query), (4, grad_attended), (6, branch)):
        s.late[row : row + 1] = exact(column_sum(values), exact_narrow, ((1,), (0,)))
    small_out[8:9] = wide_sum


def step_kernel(
    qkv_in, out_in, up_in, down_in, up_bias, gains, biases, x0_in, skip_in, cot_in, lengths, y_out, embeds_out,
    skip_out, o1, o2, small_out, acts_all, *scratch,
):
    s = Refs(lengths=lengths)
    for (name, _, _), ref in zip(step_scratch(x0_in.shape[1]), scratch):
        setattr(s, name, ref)
    x0, skip, skip_grad = s.x0, s.skip, s.skip_grad
    gather_sem, column_sem, reduce_sem, plane_sem, load_sem = scratch[-5:]
    width = x0.shape[1]
    spans = x0.shape[0] // SPAN
    y, x, c, z = place()
    wide = lax.axis_index("wide")
    me = flat(y, x, c, z)
    w0, w1, w2, upz, downz, pars = s.w0, s.w1, s.w2, s.upz, s.downz, s.pars
    loads = [
        pltpu.make_async_copy(src, dst, load_sem.at[k])
        for k, (src, dst) in enumerate(
            (
                (qkv_in, o1.at[:, :, : 3 * width]), (out_in, o1.at[:, :, 3 * width : 4 * width]),
                (up_in, o1.at[:, :, 4 * width :]), (down_in, o2), (x0_in, x0), (skip_in, skip), (cot_in, s.cot),
            )
        )
    ]
    for load in loads:
        load.start()
    greet(wide, z)
    for load in loads[:4]:
        load.wait()
    w0[me] = o1[0, :, : 4 * width].astype(jnp.bfloat16)
    w1[me] = o1[1].astype(jnp.bfloat16)
    w2[me] = o2[1].astype(jnp.bfloat16)
    upz[z] = o1[0, :, 4 * width :].astype(jnp.bfloat16)
    downz[z] = o2[0].astype(jnp.bfloat16)
    s.small_all[me] = jnp.zeros((2 * ROWS, 128), jnp.float32)
    for layer in range(2):
        r, share = ROWS * layer, width // 32
        s.small_all[me, r : r + 2, :share] = gains[layer]
        s.small_all[me, r + 2 : r + 8, :share] = biases[:, layer]
        s.small_all[me, r + 8 : r + 9, : 4 * share] = up_bias[layer : layer + 1]

    half, mid = 2 * width, w2.shape[1] // 2

    def column_pair(ref, start):
        cut = lambda at: (lambda u: ref.at[u, :, at : at + half])
        subs = [(None, cut(start), "x"), (None, cut(start + half), "y")]
        return subs, lambda n: ref.at[pl.ds(0, n), :, start : start + half]

    rows_cut = lambda at: (lambda u: w2.at[u, at : at + mid])
    sets = [
        ([(None, lambda u: s.small_all.at[u], "x")], lambda n: s.small_all.at[pl.ds(0, n)]),
        column_pair(w0, 0),
        column_pair(w1, 0),
        column_pair(w1, 2 * half),
        ([(None, rows_cut(0), "x"), (None, rows_cut(mid), "y")], lambda n: w2.at[pl.ds(0, n), :mid]),
    ]
    events = []
    drains = []
    for k, (subs, many) in enumerate(sets):
        steps, drain = gather_steps(subs, many, gather_sem.at[k])
        drains.append(drain)
        for step, action in enumerate(steps):
            events.append((SET_AT[k][step], action))
    steps, drain = column_steps(
        [lambda zz: upz.at[zz], lambda zz: downz.at[zz]],
        [lambda n: w1.at[pl.ds(0, n), :, : 2 * half], lambda n: w2.at[pl.ds(0, n)]],
        column_sem,
    )
    drains.append(drain)
    events += zip(COLUMN_AT, steps)

    def row_of(layer):
        return lambda k: pars[pl.ds(ROWS * layer + k, 1), :]

    def unpack():
        share = width // 32
        for layer in range(2):
            r = ROWS * layer
            for d in range(32):
                pars[r : r + 8, share * d : share * (d + 1)] = s.small_all[d, r : r + 8, :share]
                at = slice((d % 8) * 4 * share, (d % 8 + 1) * 4 * share)
                pars[r + 8 + d // 8 : r + 9 + d // 8, at] = s.small_all[d, r + 8 : r + 9, : 4 * share]
        pars[...] = pars[...].astype(jnp.bfloat16).astype(jnp.float32)

    def join(rows):
        row = iota(skip.shape, 0)
        joined = skip[...].astype(jnp.float32)
        for span in range(spans):
            joined = jnp.where(row == SPAN * span, rows[span : span + 1], joined)
        s.x[...] = joined.astype(jnp.bfloat16)

    def unload():
        for load in loads[4:]:
            load.wait()

    outs = []

    def put_out(src, dst):
        copy = pltpu.make_async_copy(src, dst, load_sem.at[len(outs)])
        copy.start()
        outs.append(copy)

    events += [(UNPACK_AT, unload)]
    plane = Plane(plane_sem)
    forward0 = backbone_forward(s, plane, row_of(0), join)
    forward1 = head_forward(s, w1, w2, row_of(1), lengths)
    events += [(UNPACK_AT, unpack)]
    events += [(at, lambda: next(forward0)) for at in FORWARD0_AT]
    events += [(at, lambda: next(forward1)) for at in FORWARD1_AT]
    for _, action in sorted(events, key=lambda event: event[0]):
        action()
    for drain in drains:
        drain()
    put_out(s.y, y_out)

    back1 = head_backward(s, w1, w2, w1, w2, row_of(1), s.sums, skip_grad)
    back0 = backbone_backward(
        s, plane, row_of(0),
        lambda: jnp.concatenate([skip_grad[SPAN * k : SPAN * k + 1] for k in range(spans)], axis=0),
    )

    def reduced(whole, own, out, name, dim):
        bufs = [getattr(s, name + kind) for kind in KINDS]
        return Refs(all=whole, own=own, out=out, dim=dim, sib=bufs[0], second=bufs[1], first=bufs[2], chain=bufs[3])

    def pair(ref, start, stop, out, name):
        middle = (start + stop) // 2
        cut = lambda a, b: (ref.at[:, :, a:b], lambda u: ref.at[u, :, a:b], out.at[:, a:b])
        return [
            reduced(*cut(start, middle), name + "a", "x"),
            reduced(*cut(middle, stop), name + "b", "y"),
        ]

    made = iter(range(6))
    group = lambda *subs: Reduce(subs, reduce_sem.at[next(made)])
    cut = lambda a, b: (w2.at[:, a:b], lambda u: w2.at[u, a:b], o2.at[1, a:b])
    downs = [group(reduced(*cut(0, mid), "da", "x"), reduced(*cut(mid, 2 * mid), "db", "y"))]
    ups = [group(*pair(w1, 4 * width, 8 * width, o1.at[1], "u"))]
    lefts = [
        group(*pair(w1, 0, 4 * width, o1.at[1], "q")),
        group(reduced(s.block1, lambda u: s.block1.at[u], small_out.at[ROWS : 2 * ROWS], "s1", "x")),
    ]
    kvs = [
        group(*pair(w0, width, 3 * width, o1.at[0], "k")),
        group(reduced(s.block0, lambda u: s.block0.at[u], small_out.at[0:8], "s0", "y")),
    ]
    waves = Waves([downs, ups, lefts, kvs], LAGS)

    def start(groups):
        for zz in TARGETS:
            for each in groups:
                each.start(zz)

    def fill_blocks(block, sums, wide_too):
        share = width // 32
        block[...] = jnp.zeros_like(block)
        for d in range(32):
            block[d, 0:8, :share] = sums[0:8, share * d : share * (d + 1)]
            if wide_too:
                at = slice((d % 8) * 4 * share, (d % 8 + 1) * 4 * share)
                block[d, 8:9, : 4 * share] = sums[8 + d // 8 : 9 + d // 8, at]

    def step(times):
        for _ in range(times):
            waves.step()

    next(back1)
    for chip in range(4):
        next(back1)
        for each in downs:
            each.start_chip(chip)
    next(back1)
    next(back1)
    step(STEPS[0])
    next(back1)
    next(back1)
    step(STEPS[1])
    next(back1)
    start(ups)
    next(back1)
    step(STEPS[2])
    next(back1)
    step(STEPS[3])
    next(back1)
    step(STEPS[4])
    next(back1)
    next(back0)
    step(STEPS[5])
    next(back1)
    fill_blocks(s.block1, s.sums, True)
    start(lefts)
    next(back0)
    step(STEPS[6])
    next(back0)
    step(STEPS[7])
    next(back0)
    home = lambda u: acts_all.at[u // 8, pl.ds(pl.multiple_of((u % 8) * 32, 32), 32)]
    own_acts = pltpu.make_async_copy(s.acts_low, home(me), load_sem.at[5])
    own_acts.start()
    rows = lambda n: acts_all.at[pl.ds(0, n // 16)] if n >= 16 else acts_all.at[0, pl.ds(0, ROWS * n)]
    part = lambda k: (lambda u: home(u).at[pl.ds(ROWS * k, ROWS)])
    spread, drain = gather_steps(
        [(s.acts_low.at[pl.ds(ROWS * k, ROWS)], part(k), dim) for k, dim in enumerate("xy")], rows, gather_sem.at[5]
    )
    spread[0]()
    next(back0)
    fill_blocks(s.block0, s.sums0, False)
    start(kvs)
    row = iota(skip_grad.shape, 0)
    skip_grad[...] = jnp.where(row % SPAN == 0, 0.0, skip_grad[...])
    put_out(skip_grad, skip_out)
    put_out(s.embeds_grad, embeds_out)
    left = waves.left()
    turns = left - TAIL
    for k in range(left):
        waves.step()
        if k < turns:
            for action in spread[1 + 15 * k // turns : 1 + 15 * (k + 1) // turns]:
                action()
        if k == turns - 1:
            own_acts.wait()
            load = pltpu.make_async_copy(acts_all, s.g, load_sem.at[6])
            load.start()
            load.wait()
            backbone_weight_grads(s, me, o1, o2, small_out)
    small_out[0:8] += s.late[...]
    drain()
    plane.drain()
    for copy in outs:
        copy.wait()


SET_AT = ((0, 1, 2, 3, 4, 5, 6, 7, 8, 9, 10, 11, 12, 13, 14, 15), (0, 1, 2, 3, 4, 5, 6, 7, 8, 9, 10, 11, 12, 13, 14, 15), (1.2, 8, 9, 10, 11, 12, 13, 15, 16, 17, 18, 19, 20, 21, 22, 23), (3.2, 14, 15, 16, 17, 18, 19, 22, 23, 24, 25, 26, 27, 28, 29, 30), (5.2, 20, 21, 22, 23, 24, 25, 28.0, 28.7, 29.4, 30.1, 30.8, 31.5, 32.2, 32.9, 33.6))
UNPACK_AT = 15.05
COLUMN_AT = (2.5, 4.5, 6.5, 8.5)
FORWARD0_AT = (15.3, 16.2, 18, 20, 22)
FORWARD1_AT = (23.1, 23.9, 24.7, 25.34, 30.1, 30.9, 31.7, 32.5, 33.7)
LAGS = (0, 1, 2, 3, 4)
STEPS = (1, 1, 1, 1, 1, 1, 1, 1)
TAIL = 2
KINDS = ("sib", "second", "first", "chain")


def step_scratch(width):
    low, full = jnp.bfloat16, jnp.float32
    share = width // 32
    rows = 2 * SPAN
    found = [
        ("w0", (32, share, 4 * width), low), ("upz", (4, share, 4 * width), low),
        ("downz", (4, 4 * share, width), low), ("w1", (32, share, 8 * width), low),
        ("w2", (32, 4 * share, width), low), ("small_all", (32, 2 * ROWS, 128), full),
        ("pars", (2 * ROWS, width), full), ("sums", (ROWS, width), full), ("sums0", (8, width), full),
        ("keep", (ROWS, 8, width), full), ("p0", (2, SPAN, 128), full),
        ("g0", (ROWS, width // 2), low), ("gp0", (ROWS, width // 2), full),
        ("e0_src", (ROWS, width), low), ("e0", (8, ROWS, width), low),
        ("e1_src", (8, ROWS, width // 2), full), ("e1", (8, ROWS, width // 2), full),
        ("e2_src", (2, 8, width), full), ("e2", (8, 8, width), full),
        ("e3_src", (ROWS, width), low), ("e3", (8, ROWS, width), low),
        ("e4_src", (ROWS, width), low), ("e4", (8, ROWS, width), low),
        ("e5_src", (2, 8, width), full), ("e5", (8, 8, width), full),
        ("acts", (2 * ROWS, width), full), ("acts_low", (2 * ROWS, width), low),
        ("late", (8, 128), full), ("block1", (32, ROWS, 128), full), ("block0", (32, 8, 128), full),
        ("g", (4, rows, width), low), ("gp", (4, rows, width), full),
        ("p", (2 * HEADS, SPAN, SPAN), full), ("r1", (rows, 1), full), ("r2", (rows, 1), full),
    ]
    found += [(name, (rows, width), low) for name in ("x", "q", "k", "v", "ctx", "hl", "dz", "k0", "v0", "x0", "skip", "cot", "y")]
    found += [(name, (rows, width), full) for name in ("n1", "h", "n2", "skip_grad", "embeds_grad")]
    shapes = {
        "d": ((2 * share, width), low), "u": ((share, 2 * width), low), "q": ((share, 2 * width), low),
        "k": ((share, width), low),
    }
    blocks = [(name + side, shape) for name, shape in shapes.items() for side in "ab"]
    blocks += [("s1", ((ROWS, 128), full)), ("s0", ((8, 128), full))]
    for name, (shape, dtype) in blocks:
        for kind, many in zip(KINDS, (16, 8, 4, 5)):
            found.append((name + kind, (many,) + shape, dtype))
    return found


def step_call(params, embeds, skip_tokens, cotangent, lengths):
    vmem, hbm = pl.BlockSpec(memory_space=pltpu.VMEM), pl.BlockSpec(memory_space=pl.ANY)
    rows, width = embeds.shape
    share = width // 32
    scratch = [pltpu.VMEM(shape, dtype) for _, shape, dtype in step_scratch(width)]
    scratch += [
        pltpu.SemaphoreType.DMA((6, GATHER_SEMS)),
        pltpu.SemaphoreType.DMA((2, 5)),
        pltpu.SemaphoreType.DMA((6, REDUCE_SEMS)),
        pltpu.SemaphoreType.DMA((6, 2)),
        pltpu.SemaphoreType.DMA((7,)),
    ]
    shape = jax.ShapeDtypeStruct
    return pl.pallas_call(
        step_kernel,
        out_shape=[
            shape((rows, width), jnp.bfloat16), shape((rows, width), jnp.float32),
            shape((rows, width), jnp.float32), shape((2, share, 8 * width), jnp.float32),
            shape((2, 4 * share, width), jnp.float32), shape((2 * ROWS, 128), jnp.float32),
            shape((4, rows, width), jnp.bfloat16),
        ],
        in_specs=[hbm] * 4 + [vmem] * 3 + [hbm] * 3 + [pl.BlockSpec(memory_space=pltpu.SMEM)],
        out_specs=[hbm] * 3 + [vmem] * 3 + [hbm],
        scratch_shapes=scratch,
        compiler_params=pltpu.CompilerParams(
            collective_id=1, has_side_effects=True, vmem_limit_bytes=64 * 2**20
        ),
    )(*params, embeds, skip_tokens, cotangent, lengths)


def adam_parts(parameter, first, second, gradient, decayed):
    first = beta_first * first + (1.0 - beta_first) * gradient
    second = beta_second * second + (1.0 - beta_second) * gradient * gradient
    update = first / first_fix / (jnp.sqrt(second / second_fix) + adam_epsilon)
    if decayed:
        update = update + weight_decay * parameter
    return update, first, second


def adam_kernel(*refs):
    params, moments = refs[0:7], refs[7:14]
    joined, down, small = refs[14:17]
    passed, steps, news, handed = refs[17:20], refs[20:27], refs[27:34], refs[34:37]

    def update(index, gradient):
        step, first, second = adam_parts(
            params[index][...], moments[index][0], moments[index][1], gradient, index < 4
        )
        steps[index][...] = step
        news[index][0] = first
        news[index][1] = second

    qkv, out = params[0].shape[2], params[1].shape[2]
    update(0, joined[:, :, :qkv])
    update(1, joined[:, :, qkv : qkv + out])
    update(2, joined[:, :, qkv + out :])
    update(3, down[...])

    @pl.when(pl.program_id(1) == 0)
    def _():
        for src, dst in zip(passed, handed):
            dst[...] = src[...]

    @pl.when((pl.program_id(0) == 0) & (pl.program_id(1) == 0))
    def _():
        many = small.shape[0] // 2
        for layer in range(2):
            at = layer * many
            for index, start, stop in ((4, 8, 9), (5, 0, 2), (6, 2, 8)):
                width = params[index].shape[-1]
                here = (slice(layer, layer + 1),) if index == 4 else (layer,)
                here = here if index < 6 else (slice(None), layer)
                step, first, second = adam_parts(
                    params[index][here], moments[index][(0, *here)], moments[index][(1, *here)],
                    small[at + start : at + stop, :width], False,
                )
                steps[index][here] = step
                news[index][(0, *here)] = first
                news[index][(1, *here)] = second


def adam_update(params, moments, joined, down, small, passed):
    cuts = 3 if params[0].shape[1] % 24 == 0 else 1

    def whole(a):
        return pl.BlockSpec(a.shape, lambda l, r, n=a.ndim: (0,) * n)

    def rows(a):
        return pl.BlockSpec((1, a.shape[1] // cuts, a.shape[2]), lambda l, r: (l, r, 0))

    def pairs(a):
        return pl.BlockSpec((2, 1, a.shape[2] // cuts, a.shape[3]), lambda l, r: (0, l, r, 0))

    halves = [pl.BlockSpec((a.shape[0] // 2, a.shape[1]), lambda l, r: (l, 0)) for a in passed]
    param_specs = [rows(a) for a in params[:4]] + [whole(a) for a in params[4:]]
    moment_specs = [pairs(a) for a in moments[:4]] + [whole(a) for a in moments[4:]]
    shape = lambda a: jax.ShapeDtypeStruct(a.shape, a.dtype)
    out = pl.pallas_call(
        adam_kernel,
        grid=(2, cuts),
        out_shape=[shape(a) for a in (*params, *moments, *passed)],
        in_specs=param_specs + moment_specs + [rows(joined), rows(down), whole(small)] + halves,
        out_specs=param_specs + moment_specs + halves,
        compiler_params=pltpu.CompilerParams(vmem_limit_bytes=63 * 2**20),
    )(*params, *moments, joined, down, small, *passed)
    return out[:7], out[7:14], out[14:]


def first_forward(weights, inputs, key_valid):
    qkv_w, out_w, up_w, down_w, up_b, gain_rows, biases = weights
    row_count, width = inputs.shape
    span_count = row_count // SPAN
    first = inputs.reshape(span_count, SPAN, width)[:, 0]
    mixed = jnp.dot(inputs, qkv_w[:, width:], preferred_element_type=jnp.float32)
    keys = mixed[:, :width].astype(jnp.bfloat16).reshape(span_count, SPAN, HEADS, width // HEADS)
    values = (mixed[:, width:] + biases[1]).astype(jnp.bfloat16)
    values = values.reshape(span_count, SPAN, HEADS, width // HEADS)
    queries = jnp.dot(first, qkv_w[:, :width], preferred_element_type=jnp.float32) + biases[0]
    queries = queries.astype(jnp.bfloat16).reshape(span_count, HEADS, width // HEADS)
    scores = (
        jnp.einsum("bhe,bkhe->bhk", queries, keys, preferred_element_type=jnp.float32) * score_scale
    )
    scores = jnp.where(key_valid[:, None, :], scores, masked_score)
    probs = jax.nn.softmax(scores, axis=-1)
    context = jnp.einsum(
        "bhk,bkhe->bhe", probs.astype(jnp.bfloat16), values, preferred_element_type=jnp.float32
    )
    context = context.reshape(span_count, width).astype(jnp.bfloat16)
    attended = jnp.dot(context, out_w, preferred_element_type=jnp.float32) + biases[2]
    hidden, normed_one, scale_one = normalize(
        first.astype(jnp.float32) + attended, gain_rows[0], biases[3]
    )
    hidden_low = hidden.astype(jnp.bfloat16)
    pre_gelu = jnp.dot(hidden_low, up_w, preferred_element_type=jnp.float32) + up_b
    activated = jax.nn.gelu(pre_gelu, approximate=False).astype(jnp.bfloat16)
    branch_out = jnp.dot(activated, down_w, preferred_element_type=jnp.float32) + biases[4]
    output, normed_two, scale_two = normalize(hidden + branch_out, gain_rows[1], biases[5])
    saved = (
        first, queries, keys, values, probs, context, normed_one, scale_one, hidden_low, pre_gelu,
        activated, normed_two, scale_two,
    )
    return output, saved


def first_backward(weights, inputs, saved, grad_out):
    qkv_w, out_w, up_w, down_w, up_b, gain_rows, biases = weights
    (
        first, queries, keys, values, probs, context, normed_one, scale_one, hidden_low, pre_gelu,
        activated, normed_two, scale_two,
    ) = saved
    row_count, width = inputs.shape
    span_count = row_count // SPAN
    grad_pre_two, grad_gain_two, grad_shift_two = normalize_back(
        grad_out, normed_two, scale_two, gain_rows[1]
    )
    grad_branch = grad_pre_two.astype(jnp.bfloat16)
    grad_act = dot_last(grad_branch, down_w)
    _, gelu_back = jax.vjp(lambda inner: jax.nn.gelu(inner, approximate=False), pre_gelu)
    grad_pre_gelu = gelu_back(grad_act)[0].astype(jnp.bfloat16)
    grad_hidden = grad_pre_two + dot_last(grad_pre_gelu, up_w)
    grad_pre_one, grad_gain_one, grad_shift_one = normalize_back(
        grad_hidden, normed_one, scale_one, gain_rows[0]
    )
    grad_attended = grad_pre_one.astype(jnp.bfloat16)
    grad_context = dot_last(grad_attended, out_w).astype(jnp.bfloat16)
    grad_context = grad_context.reshape(span_count, HEADS, width // HEADS)
    grad_probs = jnp.einsum(
        "bhe,bkhe->bhk", grad_context, values, preferred_element_type=jnp.float32
    )
    grad_values = jnp.einsum("bhk,bhe->bkhe", probs.astype(jnp.bfloat16), grad_context)
    grad_values = grad_values.reshape(row_count, width).astype(jnp.bfloat16)
    grad_scores = probs * (grad_probs - jnp.sum(probs * grad_probs, axis=-1, keepdims=True))
    grad_scores = grad_scores.astype(jnp.bfloat16)
    grad_queries = (
        jnp.einsum("bhk,bkhe->bhe", grad_scores, keys, preferred_element_type=jnp.float32)
        * score_scale
    )
    grad_queries = grad_queries.reshape(span_count, width).astype(jnp.bfloat16)
    grad_keys = (
        jnp.einsum("bhk,bhe->bkhe", grad_scores, queries, preferred_element_type=jnp.float32)
        * score_scale
    )
    grad_keys = grad_keys.reshape(row_count, width).astype(jnp.bfloat16)
    grad_kv = jnp.concatenate([grad_keys, grad_values], axis=1)
    grad_kv_w = dot_first(inputs, grad_kv)
    grad_inputs = dot_last(grad_kv, qkv_w[:, width:])
    grad_first = grad_pre_one + dot_last(grad_queries, qkv_w[:, :width])
    placed = jnp.pad(grad_first[:, None], ((0, 0), (0, SPAN - 1), (0, 0))).reshape(row_count, width)
    grad_inputs = grad_inputs + placed
    rows = jnp.concatenate(
        [context, grad_attended, hidden_low, grad_pre_gelu, activated, grad_branch, first, grad_queries],
        axis=1,
    )

    def total(values):
        return jnp.sum(values, axis=0, dtype=jnp.float32)

    small = (
        total(grad_pre_gelu),
        jnp.stack([grad_gain_one, grad_gain_two]),
        jnp.stack(
            [
                total(grad_queries), total(grad_values), total(grad_attended), grad_shift_one,
                total(grad_branch), grad_shift_two,
            ]
        ),
    )
    return grad_inputs, grad_kv_w, rows, small


def first_weight_grads(rows, kv_owned, at):
    width = rows.shape[1] // 16
    wide = 4 * width
    context, grad_attended = rows[:, :width], rows[:, width : 2 * width]
    hidden_low = rows[:, 2 * width : 3 * width]
    grad_pre_gelu = rows[:, 3 * width : 3 * width + wide]
    activated = rows[:, 7 * width : 11 * width]
    grad_branch = rows[:, 11 * width : 12 * width]
    first = rows[:, 12 * width : 13 * width]
    grad_queries = rows[:, 13 * width : 14 * width]
    count = kv_owned.shape[0]
    own = lambda values, many: lax.dynamic_slice_in_dim(values, at * many, many, 1)
    return (
        jnp.concatenate([dot_first(own(first, count), grad_queries), kv_owned], axis=1),
        dot_first(own(context, count), grad_attended),
        dot_first(own(hidden_low, count), grad_pre_gelu),
        dot_first(own(activated, 4 * count), grad_branch),
    )


def pack_small(up_b, gains, biases, owners):
    parts = [up_b.reshape(owners, -1)]
    for tensor in (gains, biases):
        parts.append(tensor.reshape(tensor.shape[0], owners, -1).transpose(1, 0, 2).reshape(owners, -1))
    return jnp.concatenate(parts, axis=1)


def unpack_small(packed, width):
    owners = packed.shape[0]
    share = width // owners
    up_b = packed[:, : 4 * share].reshape(4 * width)
    gains = packed[:, 4 * share : 6 * share].reshape(owners, 2, share).transpose(1, 0, 2)
    biases = packed[:, 6 * share :].reshape(owners, 6, share).transpose(1, 0, 2)
    return up_b, gains.reshape(2, width), biases.reshape(6, width)


def exchange_weights(p1, p2, small):
    both = ("wide", "narrow")
    w1 = lax.all_gather(p1, both, axis=0)
    w2 = lax.all_gather(p2, both, axis=0)
    return (w1[:, 0], w1[:, 1]), (w2[:, 0], w2[:, 1]), lax.all_gather(small, both, axis=0)


def exchange_grads(g1, g2, kv, small, rows):
    both = ("wide", "narrow")
    summed = [
        lax.psum_scatter(a, both, scatter_dimension=0).astype(jnp.float32) for a in (g1, g2, kv, small)
    ]
    return summed + [lax.all_gather(rows, both, axis=0)]


def rows_ahead(group):
    last = group[6]
    return (*group[:6], jnp.swapaxes(last, last.ndim - 3, last.ndim - 2))


def fused_step(embeds, skip_tokens, cotangent, lengths, params, moments):
    params, moments = rows_ahead(params), rows_ahead(moments)
    y, embeds_grad, skip_grad, o1, o2, small, _ = step_call(params, embeds, skip_tokens, cotangent, lengths)
    new_steps, new_moments, passed = adam_update(params, moments, o1, o2, small, (y, embeds_grad, skip_grad))
    return (*passed, *rows_ahead(new_steps), *rows_ahead(new_moments))


def per_device(
    embeds, skip_tokens, cotangent, lengths, qkv_weight, out_weight, up_weight, down_weight, up_bias,
    norm_gains, biases, qkv_moments, out_moments, up_moments, down_moments, up_bias_moments,
    gain_moments, bias_moments,
):
    params = (qkv_weight, out_weight, up_weight, down_weight, up_bias, norm_gains, biases)
    moments = (
        qkv_moments, out_moments, up_moments, down_moments, up_bias_moments, gain_moments, bias_moments,
    )
    wide_size, narrow_size = lax.axis_size("wide"), lax.axis_size("narrow")
    if (wide_size, narrow_size) == (8, 4):
        return fused_step(embeds, skip_tokens, cotangent, lengths, params, moments)
    owners = wide_size * narrow_size
    at = lax.axis_index("wide") * narrow_size + lax.axis_index("narrow")
    span_count = lengths.shape[0]
    row_count, width = embeds.shape
    positions = lax.broadcasted_iota(jnp.int32, (span_count, SPAN), 1)
    key_valid = positions < lengths[:, None]
    row_index = lax.broadcasted_iota(jnp.int32, (1, SPAN, 1), 1)

    p1 = jnp.concatenate([qkv_weight, out_weight, up_weight], axis=2).astype(jnp.bfloat16)
    p2 = down_weight.astype(jnp.bfloat16)
    share = 12 * width // owners
    tiles = -(-2 * share // 1024)
    small_own = jnp.concatenate(
        [up_bias, norm_gains.reshape(2, -1), biases.reshape(2, -1)], axis=1
    ).reshape(-1)
    small_own = jnp.pad(small_own, (0, tiles * 1024 - 2 * share)).reshape(tiles * 8, 128)
    w1, w2, small_all = exchange_weights(p1, p2, small_own)
    small_all = small_all.reshape(owners, -1)[:, : 2 * share].astype(jnp.bfloat16).astype(jnp.float32)

    def layer_weights(layer):
        joined = w1[layer].reshape(width, -1)
        return (
            joined[:, : 3 * width], joined[:, 3 * width : 4 * width], joined[:, 4 * width :],
            w2[layer].reshape(-1, width),
        ) + unpack_small(small_all[:, layer * share : (layer + 1) * share], width)

    backbone, head = layer_weights(0), layer_weights(1)
    backbone_out, saved = first_forward(backbone, embeds, key_valid)
    skip_view = skip_tokens.reshape(span_count, SPAN, width)
    head_in = jnp.where(row_index == 0, backbone_out.astype(jnp.bfloat16)[:, None], skip_view)
    head_in = head_in.reshape(row_count, width)
    head_out, grad_head_in, head_grads = backward_block(
        head, head_in, key_valid, cotangent.astype(jnp.float32)
    )
    grad_view = grad_head_in.reshape(span_count, SPAN, width)
    skip_grad = jnp.where(row_index == 0, 0.0, grad_view).reshape(row_count, width)
    embeds_grad, grad_kv_w, rows, small_first = first_backward(
        backbone, embeds, saved, grad_view[:, 0]
    )
    low = lambda a: a.astype(jnp.bfloat16)
    g1 = jnp.concatenate([low(head_grads[0]), low(head_grads[1]), low(head_grads[2])], axis=1)
    g1 = g1.reshape(owners, width // owners, -1)
    g2 = low(head_grads[3]).reshape(owners, -1, width)
    kv = low(grad_kv_w).reshape(owners, width // owners, -1)
    small_grads = jnp.concatenate(
        [pack_small(*small_first, owners), pack_small(*head_grads[4:], owners)], axis=1
    )
    small_grads = jnp.pad(small_grads, ((0, 0), (0, tiles * 1024 - 2 * share)))
    small_grads = small_grads.reshape(owners, tiles * 8, 128)
    rows_wide = jnp.pad(rows, ((0, 0), (0, 2 * width)))
    own_g1, own_g2, own_kv, own_small, all_rows = exchange_grads(
        g1, g2, kv, small_grads, rows_wide.reshape(16 * span_count // 2, -1)
    )
    all_rows = all_rows.reshape(owners * span_count, -1)
    first_grads = first_weight_grads(all_rows, own_kv, at)
    own_small = own_small.reshape(-1)[: 2 * share].reshape(2, share)
    sixth = width // owners
    joined = jnp.stack([jnp.concatenate(first_grads[:3], axis=1), own_g1])
    down = jnp.stack([first_grads[3], own_g2])
    pad = lambda a: jnp.pad(a, ((0, 0), (0, 0), (0, 128 - a.shape[2])))
    small = [
        pad(own_small[:, 4 * sixth : 6 * sixth].reshape(2, 2, sixth)),
        pad(own_small[:, 6 * sixth :].reshape(2, 6, sixth)),
        pad(own_small[:, None, : 4 * sixth]),
        jnp.zeros((2, 7, 128), jnp.float32),
    ]
    small = jnp.concatenate(small, axis=1).reshape(32, 128)
    passed = (head_out.astype(jnp.bfloat16), embeds_grad, skip_grad)
    new_steps, new_moments, passed = adam_update(
        rows_ahead(params), rows_ahead(moments), joined, down, small, passed
    )
    return (*passed, *rows_ahead(new_steps), *rows_ahead(new_moments))


def solution(mesh):
    return jax.shard_map(
        per_device,
        mesh=mesh,
        in_specs=(
            P(("wide", "narrow"), None),
            P(("wide", "narrow"), None),
            P(("wide", "narrow"), None),
            P(("wide", "narrow")),
            P(None, ("wide", "narrow"), None),
            P(None, ("wide", "narrow"), None),
            P(None, ("wide", "narrow"), None),
            P(None, ("wide", "narrow"), None),
            P(None, ("wide", "narrow")),
            P(None, None, ("wide", "narrow")),
            P(None, None, ("wide", "narrow")),
            P(None, None, ("wide", "narrow"), None),
            P(None, None, ("wide", "narrow"), None),
            P(None, None, ("wide", "narrow"), None),
            P(None, None, ("wide", "narrow"), None),
            P(None, None, ("wide", "narrow")),
            P(None, None, None, ("wide", "narrow")),
            P(None, None, None, ("wide", "narrow")),
        ),
        out_specs=(
            P(("wide", "narrow"), None),
            P(("wide", "narrow"), None),
            P(("wide", "narrow"), None),
            P(None, ("wide", "narrow"), None),
            P(None, ("wide", "narrow"), None),
            P(None, ("wide", "narrow"), None),
            P(None, ("wide", "narrow"), None),
            P(None, ("wide", "narrow")),
            P(None, None, ("wide", "narrow")),
            P(None, None, ("wide", "narrow")),
            P(None, None, ("wide", "narrow"), None),
            P(None, None, ("wide", "narrow"), None),
            P(None, None, ("wide", "narrow"), None),
            P(None, None, ("wide", "narrow"), None),
            P(None, None, ("wide", "narrow")),
            P(None, None, None, ("wide", "narrow")),
            P(None, None, None, ("wide", "narrow")),
        ),
        check_vma=False,
    )
```

profile of v0, /device:TPU:9, one launch (start us, length us, event | category | flops | bytes accessed | tf_op | source)
XLA Modules:
  0.0 226.8 jit_solution(87817259604062824)
XLA Ops:
  0.7 217.3 %shard_map.305 = (bf16[256,768]{1,0:T(8,128)(2,1)}, f32[256,768]{1,0:T(8,128)}, f32[256,768]{1,0:T(8,128)}, f32[2,24,6144]{2,1,0:T(8,128)}, f32[2,96,768]{2,1,0:...) custom-call(f32[2,24,2304]{2,1,0:T(8,128)} %refs_0_.1, f32[2,24,768]{2,1,0:T(8,128)} %refs_1_.1, ...), custom_call_target="tpu_custom_call" | custom-call | tf_op jit(solution)/shard_map/pallas_call | solution.py:1288
  218.0 8.6 %shard_map.306 = (f32[2,24,2304]{2,1,0:T(8,128)}, f32[2,24,768]{2,1,0:T(8,128)}, f32[2,24,3072]{2,1,0:T(8,128)}, f32[2,96,768]{2,1,0:T(8,128)}, f32[2,96]{1,0:T(...) custom-call(f32[2,24,2304]{2,1,0:T(8,128)} %refs_0_.1, ...), custom_call_target="tpu_custom_call" | custom-call | tf_op jit(solution)/shard_map/pallas_call | solution.py:1372
where the time goes:
time: 230 us; the launch traced here: 227 us
  Pallas kernels  226 us (98%)
    pallas_call x1, Pallas kernels, step_call(): pl.pallas_call(step_kernel, out_shape=[shape((rows, width), jnp.bfloat16)...  217 us
    pallas_call x1, Pallas kernels, adam_update(): pl.pallas_call(adam_kernel, grid=(2, cuts), out_shape=[shape(a) for a in...  8.56 us

commit v1 on v0

--- a/solution.py
+++ b/solution.py
@@ -438,9 +438,14 @@
             total = total + part[...].astype(jnp.float32)
         dst[...] = total.astype(dst.dtype)
 
+    def start_role(self, far1, far2):
+        return (1 - far2) * (2 - far1)
+
+    second_role = staticmethod(lambda far1: 3 if far1 else 4)
+
     def start(self, zz):
         for far1, far2 in ((False, True), (True, True), (True, False), (False, False)):
-            at = 6 * zz + (0 if far2 else 1 if far1 else 2)
+            at = 6 * zz + self.start_role(int(far1), int(far2))
             for sub in self.subs:
                 src, slot = self.own(sub, far1, far2, zz, 1 - self.c)
                 send(src, sub.sib.at[slot], self.sem.at[29], self.sem.at[at], self.sib)
@@ -451,7 +456,7 @@
             for sub in self.subs:
                 fy, fx = (cy + self.y) % 2, (cx + self.x) % 2
                 far1, far2 = (fx, fy) if sub.dim == "x" else (fy, fx)
-                at = 6 * zz + (1 - far2) * (2 - far1)
+                at = 6 * zz + self.start_role(far1, far2)
                 src = sub.own(flat(cy, cx, 1 - self.c, zz))
                 send(src, sub.sib.at[chip * 4 + zz], self.sem.at[29], self.sem.at[at], self.sib)
 
@@ -463,7 +468,7 @@
                 self.add(acc, sub.sib.at[slot])
                 slot = self.coord(sub, far1) * 4 + zz
                 there = self.yn if sub.dim == "x" else self.xn
-                send(acc, sub.second.at[slot], self.sem.at[30], self.sem.at[6 * zz + (3 if far1 else 4)], there)
+                send(acc, sub.second.at[slot], self.sem.at[30], self.sem.at[6 * zz + self.second_role(far1)], there)
 
     def step_b(self, zz):
         self.take(6 * zz + 1, self.subs[0].sib)
@@ -526,8 +531,83 @@
                 for sub in self.subs:
                     sub.out[...] += sub.chain[slot].astype(jnp.float32)
 
-        for at, count in ((29, 16), (30, 8), (31, 4), (32, 3)):
-            await_sent(self.subs[0].all.at[pl.ds(0, count * self.each)], self.sem.at[at])
+        self.sent(16, 8, 4, 3)
+
+    def near_finish(self):
+        pass
+
+    def sent(self, *counts):
+        for k, count in enumerate(counts):
+            await_sent(self.subs[0].all.at[pl.ds(0, count * self.each)], self.sem.at[29 + k])
+
+
+class ReduceLate(Reduce):
+    def start_role(self, far1, far2):
+        return 1 - far2
+
+    second_role = staticmethod(lambda far1: 3)
+
+    def step_b(self, zz):
+        self.take(6 * zz + 1, self.subs[0].sib, 2)
+        self.take(6 * zz + 3, self.subs[0].second, 2)
+        for far1 in (True, False):
+            for sub in self.subs:
+                acc, slot = self.own(sub, far1, False, zz, self.c)
+                self.add(acc, sub.sib.at[slot], sub.second.at[self.coord(sub, far1) * 4 + zz])
+        for up, at in ((True, 0), (False, 3)):
+            if zz != at:
+                self.pass_on(zz, up, self.z == at)
+
+    def pass_on(self, zz, up, pred):
+        z = self.z
+        slot = zz if up else jnp.where(z - 1 == zz, 4, zz)
+        there = device(self.y, self.x, self.c, z + 1 if up else z - 1)
+        for far1 in range(2):
+            for sub in self.subs:
+                acc, _ = self.own(sub, far1 == 1, False, zz, self.c)
+                send(acc, sub.chain.at[2 * slot + far1], self.sem.at[32], self.sem.at[24 + slot], there, pred)
+
+    def join(self, zz, slot):
+        self.take(24 + slot, self.subs[0].chain, 2)
+        for far1 in range(2):
+            for sub in self.subs:
+                acc, _ = self.own(sub, far1 == 1, False, zz, self.c)
+                self.add(acc, sub.chain.at[2 * slot + far1])
+
+    def relay(self, zz, at, up):
+        @pl.when(self.z == at)
+        def _():
+            self.join(zz, zz)
+            self.pass_on(zz, up, None)
+
+    def step_c(self, zz):
+        Reduce.step_d(self, zz)
+
+    def step_d(self, zz):
+        Reduce.step_e(self, zz)
+
+    def step_e(self, zz):
+        pass
+
+    def near_finish(self):
+        z = self.z
+        for pred, slot in ((z > 0, z), (z < 3, 4)):
+
+            @pl.when(pred)
+            def _(slot=slot):
+                self.join(z, slot)
+
+        for sub in self.subs:
+            acc, _ = self.own(sub, True, False, z, self.c)
+            there = self.xn if sub.dim == "x" else self.yn
+            send(acc, sub.first.at[0], self.sem.at[31], self.sem.at[5], there)
+
+    def finish(self):
+        self.take(5, self.subs[0].first)
+        for sub in self.subs:
+            acc, _ = self.own(sub, False, False, self.z, self.c)
+            sub.out[...] = acc[...].astype(jnp.float32) + sub.first[0].astype(jnp.float32)
+        self.sent(16, 8, 1, 6)
 
 
 class Waves:
@@ -537,21 +617,22 @@
         self.at = 0
 
     def step(self):
-        stages = (Reduce.step_a, Reduce.step_b, Reduce.step_c, Reduce.step_d, Reduce.step_e)
+        stages = ("step_a", "step_b", "step_c", "step_d", "step_e")
         for lag, stage in zip(self.lags, stages):
             k = self.at - lag
             if 0 <= k < len(self.waves):
                 group, zz = self.waves[k]
                 for made in group:
-                    stage(made, zz)
-        k = self.at - self.lags[-1] - 1
-        if 0 <= k < len(self.waves) and k % 4 == 3:
-            for made in self.waves[k][0]:
-                made.finish()
+                    getattr(made, stage)(zz)
+        for more, stage in ((1, "near_finish"), (2, "finish")):
+            k = self.at - self.lags[-1] - more
+            if 0 <= k < len(self.waves) and k % 4 == 3:
+                for made in self.waves[k][0]:
+                    getattr(made, stage)()
         self.at += 1
 
     def left(self):
-        return len(self.waves) + self.lags[-1] + 1 - self.at
+        return len(self.waves) + self.lags[-1] + 2 - self.at
 
 
 def erf_of(v):
@@ -1128,9 +1209,10 @@
 
     made = iter(range(6))
     group = lambda *subs: Reduce(subs, reduce_sem.at[next(made)])
+    group_late = lambda *subs: ReduceLate(subs, reduce_sem.at[next(made)])
     cut = lambda a, b: (w2.at[:, a:b], lambda u: w2.at[u, a:b], o2.at[1, a:b])
-    downs = [group(reduced(*cut(0, mid), "da", "x"), reduced(*cut(mid, 2 * mid), "db", "y"))]
-    ups = [group(*pair(w1, 4 * width, 8 * width, o1.at[1], "u"))]
+    downs = [group_late(reduced(*cut(0, mid), "da", "x"), reduced(*cut(mid, 2 * mid), "db", "y"))]
+    ups = [group_late(*pair(w1, 4 * width, 8 * width, o1.at[1], "u"))]
     lefts = [
         group(*pair(w1, 0, 4 * width, o1.at[1], "q")),
         group(reduced(s.block1, lambda u: s.block1.at[u], small_out.at[ROWS : 2 * ROWS], "s1", "x")),
@@ -1230,8 +1312,8 @@
 COLUMN_AT = (2.5, 4.5, 6.5, 8.5)
 FORWARD0_AT = (15.3, 16.2, 18, 20, 22)
 FORWARD1_AT = (23.1, 23.9, 24.7, 25.34, 30.1, 30.9, 31.7, 32.5, 33.7)
-LAGS = (0, 1, 2, 3, 4)
-STEPS = (1, 1, 1, 1, 1, 1, 1, 1)
+LAGS = (0, 2, 4, 6, 8)
+STEPS = (2, 2, 1, 1, 1, 1, 2, 2)
 TAIL = 2
 KINDS = ("sib", "second", "first", "chain")
 
@@ -1267,7 +1349,7 @@
     blocks = [(name + side, shape) for name, shape in shapes.items() for side in "ab"]
     blocks += [("s1", ((ROWS, 128), full)), ("s0", ((8, 128), full))]
     for name, (shape, dtype) in blocks:
-        for kind, many in zip(KINDS, (16, 8, 4, 5)):
+        for kind, many in zip(KINDS, (16, 8, 2, 10) if name[0] in "du" else (16, 8, 4, 5)):
             found.append((name + kind, (many,) + shape, dtype))
     return found
 

time: 230 us -> 223 us (0.970)
  the two profiles are of different devices: /device:TPU:9 before, /device:TPU:17 now
where the time goes in v1:
time: 223 us; the launch traced here: 220 us
  Pallas kernels  220 us (99%)
    pallas_call x1, Pallas kernels, step_call(): pl.pallas_call(step_kernel, out_shape=[shape((rows, width), jnp.bfloat16)...  211 us
    pallas_call x1, Pallas kernels, adam_update(): pl.pallas_call(adam_kernel, grid=(2, cuts), out_shape=[shape(a) for a in...  8.56 us

profile of v1, /device:TPU:17, one launch (start us, length us, event | category | flops | bytes accessed | tf_op | source)
XLA Modules:
  0.0 220.4 jit_solution(16774033171933732927)
XLA Ops:
  0.7 211.0 %shard_map.305 = (bf16[256,768]{1,0:T(8,128)(2,1)}, f32[256,768]{1,0:T(8,128)}, f32[256,768]{1,0:T(8,128)}, f32[2,24,6144]{2,1,0:T(8,128)}, f32[2,96,768]{2,1,0:...) custom-call(f32[2,24,2304]{2,1,0:T(8,128)} %refs_0_.1, f32[2,24,768]{2,1,0:T(8,128)} %refs_1_.1, ...), custom_call_target="tpu_custom_call" | custom-call | tf_op jit(solution)/shard_map/pallas_call | solution.py:1370
  211.7 8.6 %shard_map.306 = (f32[2,24,2304]{2,1,0:T(8,128)}, f32[2,24,768]{2,1,0:T(8,128)}, f32[2,24,3072]{2,1,0:T(8,128)}, f32[2,96,768]{2,1,0:T(8,128)}, f32[2,96]{1,0:T(...) custom-call(f32[2,24,2304]{2,1,0:T(8,128)} %refs_0_.1, ...), custom_call_target="tpu_custom_call" | custom-call | tf_op jit(solution)/shard_map/pallas_call | solution.py:1454

commit v2 on v1

--- a/solution.py
+++ b/solution.py
@@ -1307,12 +1307,18 @@
         copy.wait()
 
 
-SET_AT = ((0, 1, 2, 3, 4, 5, 6, 7, 8, 9, 10, 11, 12, 13, 14, 15), (0, 1, 2, 3, 4, 5, 6, 7, 8, 9, 10, 11, 12, 13, 14, 15), (1.2, 8, 9, 10, 11, 12, 13, 15, 16, 17, 18, 19, 20, 21, 22, 23), (3.2, 14, 15, 16, 17, 18, 19, 22, 23, 24, 25, 26, 27, 28, 29, 30), (5.2, 20, 21, 22, 23, 24, 25, 28.0, 28.7, 29.4, 30.1, 30.8, 31.5, 32.2, 32.9, 33.6))
-UNPACK_AT = 15.05
+def set_at(own, rest, late):
+    return (own, *(rest + k for k in range(6)), *(late + 0.5 * k for k in range(9)))
+
+
+SET_AT = (
+    set_at(0, 1, 7), set_at(0, 1, 7), set_at(0.1, 6.2, 12.6), set_at(0.2, 11.2, 17.6), set_at(0.3, 16.2, 22.6)
+)
+UNPACK_AT = 11.05
 COLUMN_AT = (2.5, 4.5, 6.5, 8.5)
-FORWARD0_AT = (15.3, 16.2, 18, 20, 22)
-FORWARD1_AT = (23.1, 23.9, 24.7, 25.34, 30.1, 30.9, 31.7, 32.5, 33.7)
-LAGS = (0, 2, 4, 6, 8)
+FORWARD0_AT = (11.3, 12.2, 14.0, 16.0, 18.0)
+FORWARD1_AT = (18.1, 18.9, 19.7, 20.34, 21.7, 22.5, 23.3, 24.1, 26.7)
+LAGS = (0, 2, 5, 7, 9)
 STEPS = (2, 2, 1, 1, 1, 1, 2, 2)
 TAIL = 2
 KINDS = ("sib", "second", "first", "chain")

time: 223 us -> 213 us (0.955)
  the two profiles are of different devices: /device:TPU:17 before, /device:TPU:9 now
where the time goes in v2:
time: 213 us; the launch traced here: 209 us
  Pallas kernels  208 us (98%)
    pallas_call x1, Pallas kernels, step_call(): pl.pallas_call(step_kernel, out_shape=[shape((rows, width), jnp.bfloat16)...  199 us
    pallas_call x1, Pallas kernels, adam_update(): pl.pallas_call(adam_kernel, grid=(2, cuts), out_shape=[shape(a) for a in...  8.56 us

profile of v2, /device:TPU:9, one launch (start us, length us, event | category | flops | bytes accessed | tf_op | source)
XLA Modules:
  0.0 208.8 jit_solution(5146790959782420531)
XLA Ops:
  0.7 199.4 %shard_map.305 = (bf16[256,768]{1,0:T(8,128)(2,1)}, f32[256,768]{1,0:T(8,128)}, f32[256,768]{1,0:T(8,128)}, f32[2,24,6144]{2,1,0:T(8,128)}, f32[2,96,768]{2,1,0:...) custom-call(f32[2,24,2304]{2,1,0:T(8,128)} %refs_0_.1, f32[2,24,768]{2,1,0:T(8,128)} %refs_1_.1, ...), custom_call_target="tpu_custom_call" | custom-call | tf_op jit(solution)/shard_map/pallas_call | solution.py:1376
  200.1 8.6 %shard_map.306 = (f32[2,24,2304]{2,1,0:T(8,128)}, f32[2,24,768]{2,1,0:T(8,128)}, f32[2,24,3072]{2,1,0:T(8,128)}, f32[2,96,768]{2,1,0:T(8,128)}, f32[2,96]{1,0:T(...) custom-call(f32[2,24,2304]{2,1,0:T(8,128)} %refs_0_.1, ...), custom_call_target="tpu_custom_call" | custom-call | tf_op jit(solution)/shard_map/pallas_call | solution.py:1460
